TPU v7x, 32 devices: a whole 2x2x4 slice. The times are simulated.
32 devices in a mesh: groups: 1, expert: 16 (over z, y, x), shard: 2 (over core).
Axes of the slice: x: 2, y: 2, z: 4, core: 2. Of those that a mesh axis runs over, the one named last changes fastest.
Arguments:
- tokens: bfloat16 [256, 4096], P(('groups', 'expert'), 'shard'), may hold values from -6 to 6
- gate_scale: float32 [256, 8], P(('groups', 'expert')), may hold values from 0.2 to 1
- expert_ids: int32 [256, 8], P(('groups', 'expert')), may hold values from 0 to 15, all different within a row; in each aligned block of 16 rows (0 to 15, 16 to 31, ...) at most 16 rows name the same one
- latent_in: bfloat16 [4096, 1024], P(None, 'expert'), may hold values from -0.09375 to 0.09375
- latent_out: bfloat16 [1024, 4096], P(('expert', 'shard')), may hold values from -0.375 to 0.375
- moe_gate: bfloat16 [16, 1024, 1536], P('expert', None, 'shard'), may hold values from -0.1875 to 0.1875
- moe_up: bfloat16 [16, 1024, 1536], P('expert', None, 'shard'), may hold values from -0.1875 to 0.1875
- moe_down: bfloat16 [16, 1536, 1024], P('expert', 'shard'), may hold values from -0.15625 to 0.15625
- shared_gate: bfloat16 [4096, 8192], P(None, ('expert', 'shard')), may hold values from -0.09375 to 0.09375
- shared_up: bfloat16 [4096, 8192], P(None, ('expert', 'shard')), may hold values from -0.09375 to 0.09375
- shared_down: bfloat16 [8192, 4096], P(('expert', 'shard')), may hold values from -0.125 to 0.125
Outputs:
- mixed: bfloat16 [256, 4096], P(('groups', 'expert'), 'shard')
Inputs may be any that keep to these rules, and one draw needn't show every extreme that they name: `expert_ids`: each row names 8 different experts. In each aligned block of 16 rows (the rows of one index of expert) no expert is named by more than 16 rows.
All inputs are finite; a program needn't handle non-finite values.
Results may differ from a plain program's by a relative error of at most 0.0075.
Values may be sent and summed in bfloat16 or wider, within the bound.
A program may use at most 128 MiB of HBM per device.

v0:
```python
import jax
import jax.numpy as jnp
from jax import lax
from jax.sharding import PartitionSpec as P


def per_device(
    tokens,
    gate_scale,
    expert_ids,
    latent_in,
    latent_out,
    moe_gate,
    moe_up,
    moe_down,
    shared_gate,
    shared_up,
    shared_down,
):
    n_exp = lax.axis_size("expert")
    tok = tokens.shape[0]
    top = expert_ids.shape[1]
    width = latent_in.shape[0]
    half = width // 2
    lat = latent_in.shape[1] * n_exp
    cap = min(tok, 2 * tok * top // n_exp)
    full_rows = lax.all_gather(tokens, "shard", axis=1, tiled=True)
    every_token = lax.all_gather(full_rows, "expert", axis=0, tiled=True)
    column_part = jnp.dot(every_token, latent_in, preferred_element_type=jnp.float32).astype(
        jnp.bfloat16
    )
    latent = lax.all_to_all(column_part, "expert", split_axis=0, concat_axis=1, tiled=True)
    gate_s = jnp.dot(every_token, shared_gate, preferred_element_type=jnp.float32)
    up_s = jnp.dot(every_token, shared_up, preferred_element_type=jnp.float32)
    shared_hidden = (jax.nn.silu(gate_s) * up_s).astype(jnp.bfloat16)
    flat_ids = expert_ids.reshape(-1)
    onehot = (flat_ids[:, None] == jnp.arange(n_exp, dtype=jnp.int32)[None, :]).astype(jnp.int32)
    before = jnp.cumsum(onehot, axis=0) - onehot
    position = jnp.sum(before * onehot, axis=1)
    slot = flat_ids * cap + position
    place = (slot[:, None] == jnp.arange(n_exp * cap, dtype=jnp.int32)[None, :]).astype(jnp.float32)
    place = place.reshape(tok, top, n_exp * cap)
    pick = jnp.sum(place, axis=1).astype(jnp.bfloat16)
    weights = jnp.sum(place * gate_scale[:, :, None], axis=1)
    send = jnp.dot(pick.T, latent, preferred_element_type=jnp.float32).astype(jnp.bfloat16)
    send = send.reshape(n_exp, cap, lat)
    rows = lax.all_to_all(send, "expert", split_axis=0, concat_axis=0, tiled=True)
    flat = rows.reshape(-1, lat)
    gate_v = jnp.dot(flat, moe_gate[0], preferred_element_type=jnp.float32)
    up_v = jnp.dot(flat, moe_up[0], preferred_element_type=jnp.float32)
    hidden = (jax.nn.silu(gate_v) * up_v).astype(jnp.bfloat16)
    part = jnp.dot(hidden, moe_down[0], preferred_element_type=jnp.float32)
    partial_value = part.reshape(rows.shape[0], rows.shape[1], lat)
    back = lax.all_to_all(partial_value, "expert", split_axis=0, concat_axis=0, tiled=True)
    summed = lax.psum(back, "shard")
    outputs = summed.astype(jnp.bfloat16).astype(jnp.float32).reshape(-1, lat)
    routed = jnp.dot(
        weights, outputs, precision=lax.Precision.HIGHEST, preferred_element_type=jnp.float32
    ).astype(jnp.bfloat16)
    routed_cols = lax.all_to_all(routed, "expert", split_axis=1, concat_axis=0, tiled=True)
    own_width = latent_out.shape[0]
    mine = lax.dynamic_slice_in_dim(routed_cols, lax.axis_index("shard") * own_width, own_width, 1)
    combined = jnp.concatenate([shared_hidden, mine], axis=1)
    weights_cat = jnp.concatenate([shared_down, latent_out], axis=0)
    block = 2 * tok
    span = min(tok * lax.axis_size(("expert", "shard")) // block + 2, n_exp)
    rows = combined
    full = jnp.dot(rows, weights_cat, preferred_element_type=jnp.float32)
    arranged = full.reshape(span, tok, 2, half).transpose(0, 2, 1, 3).reshape(span * block, half)
    total = lax.psum_scatter(arranged, ("expert", "shard"), scatter_dimension=0, tiled=True)
    return total.astype(jnp.bfloat16)


def solution(mesh):
    placed = (
        P(("groups", "expert"), "shard"),
        P(("groups", "expert"), None),
        P(("groups", "expert"), None),
        P(None, "expert"),
        P(("expert", "shard"), None),
        P("expert", None, "shard"),
        P("expert", None, "shard"),
        P("expert", "shard", None),
        P(None, ("expert", "shard")),
        P(None, ("expert", "shard")),
        P(("expert", "shard"), None),
    )
    return jax.shard_map(
        per_device,
        mesh=mesh,
        in_specs=placed,
        out_specs=P(("groups", "expert"), "shard"),
        check_vma=False,
    )
```

profile of v0, /device:TPU:0, one launch (start us, length us, event | category | flops | bytes accessed | tf_op | source)
XLA Modules:
  0.0 325.2 jit_solution(10588920767665320902)
XLA Ops:
  6.5 0.0 copy-start
  6.5 0.0 all-gather.2.cloned.1.call-start
  6.5 3.9 %all_gather.6 = bf16[16,4096]{1,0:T(8,128)(2,1)} all-gather(bf16[16,2048]{1,0:T(8,128)(2,1)} %param.11), channel_id=1, replica_groups=mesh['groups'=1,'expert'=16,'shard'=2] {'shard'}, dimensions={1}, use_global_device_ids=true | all-gather | bytes 196608 | tf_op jit(solution)/shard_map/all_gather | solution.py:27
  10.5 0.0 all-gather.2.cloned.1.call-update
  10.5 0.8 copy.25
  11.2 0.1 eq.29
  11.3 0.8 copy.27
  12.1 0.1 fusion.20
  12.2 0.2 reduce_window_sum.11
  12.4 0.2 select_reduce_fusion.1
  12.5 0.1 reduce_sum.30
  12.6 61.1 %all-gather.2.cloned.1.call-done = bf16[256,4096]{1,0:T(8,128)(2,1)} async-done(((bf16[16,4096]{1,0:T(8,128)(2,1)}), bf16[256,4096]{1,0:T(8,128)(2,1)}) %all-gather.2.cloned.1.call-update) | async-done | bytes 2097168 | tf_op jit(solution)/shard_map/all_gather | solution.py:28
  73.8 2.4 convolution_convert_fusion.2
  76.2 0.1 copy.28
  76.3 0.7 reshape.49
  77.0 4.3 %all-to-all-start = ((bf16[16,2,512]{2,1,0:T(2,128)(2,1)}), bf16[16,2,512]{2,1,0:T(2,128)(2,1)S(1)}, u32[]{:S(2)}, u32[]{:S(2)}) async-start(bf16[16,2,512]{2,1,0:T(2,128)(2,1)} %reshape.49), calls=%async_computation | async-start | bytes 65536 | tf_op jit(solution)/shard_map/all_to_all | solution.py:32
  81.3 0.1 convert_reduce_fusion
  81.5 7.2 %all-to-all-done = bf16[16,2,512]{2,1,0:T(2,128)(2,1)S(1)} async-done(((bf16[16,2,512]{2,1,0:T(2,128)(2,1)}), bf16[16,2,512]{2,1,0:T(2,128)(2,1)S(1)}, u32[]{:S(2)}, u32[]{:S(2)}) %all-to-all-start) | async-done | bytes 32800 | tf_op jit(solution)/shard_map/all_to_all | solution.py:32
  88.7 0.1 reshape.50
  88.9 0.1 all_to_all.37
  89.0 0.3 convolution_convert_fusion
  89.3 0.0 copy-start.3
  89.3 16.2 %all_to_all.48 = bf16[16,16,1024]{2,1,0:T(8,128)(2,1)S(1)} all-to-all(bf16[16,16,1024]{2,1,0:T(8,128)(2,1)S(1)} %bitcast.45), channel_id=1, replica_groups=mesh['groups'=1,'expert'=16,'shard'=2] {'expert'}, dimensions={0} | all-to-all | bytes 1048576 | tf_op jit(solution)/shard_map/all_to_all | solution.py:47
  105.5 2.0 fusion.8
  107.5 0.0 copy-done.3
  107.5 0.0 copy-start.1
  107.5 0.6 fusion.13
  108.1 0.8 copy-done.1
  108.9 1.6 fusion.4
  110.5 3.8 %all-to-all-start.2 = ((f32[16,16,1024]{2,1,0:T(8,128)}), f32[16,16,1024]{2,1,0:T(8,128)S(1)}, u32[]{:S(2)}, u32[]{:S(2)}) async-start(f32[16,16,1024]{2,1,0:T(8,128)} %fusion.4), calls=%async_computation.2 | async-start | bytes 2097152 | tf_op jit(solution)/shard_map/all_to_all | solution.py:54
  114.3 0.0 copy-done
  114.3 2.5 fusion.23
  116.8 20.4 %all-to-all-done.2 = f32[16,16,1024]{2,1,0:T(8,128)S(1)} async-done(((f32[16,16,1024]{2,1,0:T(8,128)}), f32[16,16,1024]{2,1,0:T(8,128)S(1)}, u32[]{:S(2)}, u32[]{:S(2)}) %all-to-all-start.2) | async-done | bytes 1048608 | tf_op jit(solution)/shard_map/all_to_all | solution.py:54
  137.2 6.6 %all-reduce.1 = bf16[16,16,1024]{2,1,0:T(8,128)(2,1)} all-reduce(f32[16,16,1024]{2,1,0:T(8,128)S(1)} %all-to-all-done.2), channel_id=1, replica_groups=mesh['groups'=1,'expert'=16,'shard'=2] {'shard'}, use_global_device_ids=true, to_apply=%region_4.5 | all-reduce | flops 262144 | bytes 1572864 | tf_op jit(solution)/shard_map/psum | solution.py:55
  143.8 1.4 convolution_convert_fusion.1
  145.2 0.1 all_to_all.40
  145.3 0.7 reshape.51
  146.0 6.0 %all-to-all-start.3 = ((bf16[16,2,512]{2,1,0:T(2,128)(2,1)}), bf16[16,2,512]{2,1,0:T(2,128)(2,1)S(1)}, u32[]{:S(2)}, u32[]{:S(2)}) async-start(bf16[16,2,512]{2,1,0:T(2,128)(2,1)} %reshape.51), calls=%async_computation.3 | async-start | bytes 65536 | tf_op jit(solution)/shard_map/all_to_all | solution.py:60
  152.1 0.0 copy-start.2
  152.1 0.2 reduce-scatter.2.cloned.1.call-start
  152.3 3.2 fusion.16
  155.5 4.0 %all-to-all-done.3 = bf16[16,2,512]{2,1,0:T(2,128)(2,1)S(1)} async-done(((bf16[16,2,512]{2,1,0:T(2,128)(2,1)}), bf16[16,2,512]{2,1,0:T(2,128)(2,1)S(1)}, u32[]{:S(2)}, u32[]{:S(2)}) %all-to-all-start.3) | async-done | bytes 32800 | tf_op jit(solution)/shard_map/all_to_all | solution.py:60
  159.5 0.1 reshape.52
  159.6 0.1 constant_dynamic-slice_fusion
  159.7 0.1 copy.33
  159.7 0.0 copy-done.2
  159.8 4.8 %fusion = f32[256,4096]{1,0:T(8,128)} fusion(bf16[32,4096]{1,0:T(8,128)(2,1)S(1)} %copy-done.2, bf16[256,4096]{1,0:T(8,128)(2,1)} %param.21, bf16[256,32]{0,1:T(8,128)(2,1)S(1)} %copy.33, bf16[256,256]{0,1:T(8,128)(2,1)S(1)} %fusion.16), kind=kOutput, calls=%fused_computation | convolution fusion | flops 608993280 | bytes 6701056 | tf_op jit(solution)/shard_map/dot_general | solution.py:68
  164.6 6.6 %reshape.46 = f32[16,16,2,2048]{3,2,1,0:T(2,128)} reshape(f32[256,4096]{1,0:T(8,128)} %fusion) | data formatting | bytes 8388608 | tf_op jit(solution)/shard_map/reshape | solution.py:69
  171.2 7.4 %copy.32 = f32[16,2,16,2048]{3,2,1,0:T(8,128)} copy(f32[16,2,16,2048]{3,1,2,0:T(2,128)} %bitcast.43) | data formatting | bytes 8388608 | tf_op jit(solution)/shard_map/transpose | solution.py:69
  178.6 0.0 reduce-scatter.2.cloned.1.call-update
  178.6 138.2 %reduce-scatter.2.cloned.1.call-done = f32[16,2048]{1,0:T(8,128)} async-done(((f32[512,2048]{1,0:T(8,128)}), f32[16,2048]{1,0:T(8,128)}) %reduce-scatter.2.cloned.1.call-update) | async-done | bytes 131088 | tf_op jit(solution)/shard_map/reduce_scatter | solution.py:70
  316.9 1.5 convert_element_type.41
  (3 shorter events, 0.1 us)
Async XLA Ops:
  6.5 107.8 %copy-start = (bf16[4096,256]{1,0:T(8,128)(2,1)S(1)}, bf16[4096,256]{1,0:T(8,128)(2,1)}, u32[]{:S(2)}) copy-start(bf16[4096,256]{1,0:T(8,128)(2,1)} %param.19) | copy-start | bytes 6291460
  6.5 67.2 %all-gather.2.cloned.1.call-start = ((), (), s32[]{:S(2)}) async-start(), calls=%async_computation.5 | async-start | bytes 2228224 | tf_op jit(solution)/shard_map/all_gather | solution.py:28
  77.0 11.7 %all-to-all-start = ((bf16[16,2,512]{2,1,0:T(2,128)(2,1)}), bf16[16,2,512]{2,1,0:T(2,128)(2,1)S(1)}, u32[]{:S(2)}, u32[]{:S(2)}) async-start(bf16[16,2,512]{2,1,0:T(2,128)(2,1)} %reshape.49), calls=%async_computation | async-start | bytes 65536 | tf_op jit(solution)/shard_map/all_to_all | solution.py:32
  89.3 18.2 %copy-start.3 = (bf16[1,1024,768]{2,1,0:T(8,128)(2,1)S(1)}, bf16[1,1024,768]{2,1,0:T(8,128)(2,1)}, u32[]{:S(2)}) copy-start(bf16[1,1024,768]{2,1,0:T(8,128)(2,1)} %param.17) | copy-start | bytes 4718596
  107.5 1.4 copy-start.1
  110.5 26.7 %all-to-all-start.2 = ((f32[16,16,1024]{2,1,0:T(8,128)}), f32[16,16,1024]{2,1,0:T(8,128)S(1)}, u32[]{:S(2)}, u32[]{:S(2)}) async-start(f32[16,16,1024]{2,1,0:T(8,128)} %fusion.4), calls=%async_computation.2 | async-start | bytes 2097152 | tf_op jit(solution)/shard_map/all_to_all | solution.py:54
  146.0 13.4 %all-to-all-start.3 = ((bf16[16,2,512]{2,1,0:T(2,128)(2,1)}), bf16[16,2,512]{2,1,0:T(2,128)(2,1)S(1)}, u32[]{:S(2)}, u32[]{:S(2)}) async-start(bf16[16,2,512]{2,1,0:T(2,128)(2,1)} %reshape.51), calls=%async_computation.3 | async-start | bytes 65536 | tf_op jit(solution)/shard_map/all_to_all | solution.py:60
  152.1 7.7 %copy-start.2 = (bf16[32,4096]{1,0:T(8,128)(2,1)S(1)}, bf16[32,4096]{1,0:T(8,128)(2,1)}, u32[]{:S(2)}) copy-start(bf16[32,4096]{1,0:T(8,128)(2,1)} %param.15) | copy-start | bytes 786436
  152.1 164.8 %reduce-scatter.2.cloned.1.call-start = ((), (), s32[]{:S(2)}) async-start(), calls=%async_computation.6 | async-start | bytes 4325376 | tf_op jit(solution)/shard_map/reduce_scatter | solution.py:70
Sparse Core Ops, SparseCore 0:
  10.6 63.1 all-gather.1
  178.7 138.0 reduce-scatter.1
where the time goes:
time: 326 us; the launch traced here: 325 us
  waiting for transfers between devices  231 us (71%)
  blocking collectives  26.7 us (8%)
  local copies, waits for them, and re-layouts  18.7 us (6%)
  matrix products  18.7 us (6%)
  starting transfers between devices  14.3 us (4%)
  between operations  13.6 us (4%)
    reduce_scatter x1, waiting for transfers between devices, per_device(): lax.psum_scatter(arranged, ('expert', 'shard'), scatter_dimension=0, tile...  138 us
    all_gather x1, waiting for transfers between devices, per_device(): every_token = lax.all_gather(full_rows, 'expert', axis=0, tiled=True)  61.1 us
    all_to_all x1, waiting for transfers between devices, per_device(): lax.all_to_all(partial_value, 'expert', split_axis=0, concat_axis=0, tile...  20.4 us
    all_to_all x1, blocking collectives, per_device(): lax.all_to_all(send, 'expert', split_axis=0, concat_axis=0, tiled=True)  16.2 us
    transpose x1, local copies, waits for them, and re-layouts, per_device(): full.reshape(span, tok, 2, half).transpose(0, 2, 1, 3)  7.41 us
    all_to_all x1, waiting for transfers between devices, per_device(): lax.all_to_all(column_part, 'expert', split_axis=0, concat_axis=1, tiled=...  7.25 us
    psum x1, blocking collectives, per_device(): summed = lax.psum(back, 'shard')  6.6 us
    reshape x1, local copies, waits for them, and re-layouts, per_device(): full.reshape(span, tok, 2, half).transpose(0, 2, 1, 3)  6.58 us
  transfers between devices with their start and end apart: 5, of which 5 were waited for; matrix products, arithmetic and copies ran while one was open for 2% of the time, Pallas kernels for 0%

commit v1 on v0

v1 whole, which is shorter than its diff:
```python
import functools

import jax
import jax.numpy as jnp
from jax import lax
from jax.experimental import pallas as pl
from jax.experimental.pallas import tpu as pltpu
from jax.sharding import PartitionSpec as P

MESH = pl.DeviceIdType.MESH
F32 = jnp.float32
BF16 = jnp.bfloat16
EXTRA = 128


def mm(a, b):
    return jnp.dot(a, b, preferred_element_type=F32)


def silu(v):
    return v / (1.0 + jnp.exp(-v))


def kernel(
    n_exp, plane, chunks,
    tokens, scale, ids, latent_in, latent_out, moe_gate, moe_up, moe_down,
    shared_gate, shared_up, shared_down,
    out,
    tok, li, lo, mg, mu, md, sg, su, sd,
    lat_t, lat, hid, sh, out_t, partial,
    mS, mrS, mB, mrB, mA, mrA, mZ, mrZ,
    fS, frS, fB, frB, fA, frA, fZ, frZ,
    load_sem,
    tz, ta, tb, ts, lz, la, lb, ls,
    ms, mb, ma, mz, fs, fb, fa, fz,
):
    nz = n_exp // plane
    npos = plane
    e = lax.axis_index("expert")
    s = lax.axis_index("shard")
    rows = tokens.shape[0]
    half = tokens.shape[1]
    total = rows * n_exp
    part = total // 2
    hidden = mg.shape[2]
    z, q = e // plane, e % plane
    if plane == 4:
        x, y = q % 2, q // 2
        qx, qy = q + 1 - 2 * x, q + 2 - 4 * y
        q_a = (1 - s) * qx + s * qy
        q_b = (1 - s) * qy + s * qx
        spots = [q, q_a, q_b, 3 - q]
    else:
        spots = [q]

    def at(d, j):
        return lax.rem(z - d + nz, nz) * plane + spots[j]

    def z_peer(d):
        return {"expert": lax.rem(z + d + nz, nz) * plane + q, "shard": s}

    sibling = {"expert": e, "shard": 1 - s}
    if plane == 4:
        peer_a = {"expert": z * plane + q_a, "shard": s}
        peer_b = {"expert": z * plane + q_b, "shard": s}

    loads = {}
    order = [
        ("tok", tokens, tok.at[s, pl.ds(pl.multiple_of(e * rows, rows), rows), pl.ds(0, half)]),
        ("li", latent_in, li), ("sg", shared_gate, sg), ("su", shared_up, su),
        ("mg", moe_gate, mg), ("mu", moe_up, mu), ("md", moe_down, md),
        ("sd", shared_down, sd), ("lo", latent_out, lo),
    ]
    for i, (name, src, dst) in enumerate(order):
        loads[name] = pltpu.make_async_copy(src, dst, load_sem.at[i])
        loads[name].start()

    barrier = pltpu.get_barrier_semaphore()
    peers = [z_peer(d) for d in range(1, nz)] + [sibling]
    if plane == 4:
        peers += [peer_a, peer_b]
    for peer in peers:
        pl.semaphore_signal(barrier, inc=1, device_id=peer, device_id_type=MESH)

    lane = lax.broadcasted_iota(jnp.int32, (rows, EXTRA), 1)
    weight = jnp.zeros((rows, EXTRA), F32)
    for k in range(ids.shape[1]):
        weight += jnp.where(lane == ids[:, k : k + 1], scale[:, k : k + 1], 0.0)
    high = weight.astype(BF16)
    low = (weight - high.astype(F32)).astype(BF16)
    first = jnp.broadcast_to(s, (rows, EXTRA)) == 0
    mine = jnp.where(first, high.astype(F32), low.astype(F32)).astype(BF16)
    tok[s, pl.ds(pl.multiple_of(e * rows, rows), rows), pl.ds(half, EXTRA)] = mine
    loads["tok"].wait()
    pl.semaphore_wait(barrier, len(peers))

    def copy(src, dst, sems, index, peer):
        return pltpu.make_async_remote_copy(
            src_ref=src, dst_ref=dst, send_sem=sems.at[(0,) + index],
            recv_sem=sems.at[(1,) + index], device_id=peer, device_id_type=MESH,
        )

    def gather(buf, r, zs, as_, bs, ss):
        sent = []

        def block(d, j, core):
            return buf.at[core, pl.ds(pl.multiple_of(at(d, j) * r, r), r)]

        def send(d, j, sems, index, peer):
            b = block(d, j, s)
            c = copy(b, b, sems, index, peer)
            c.start()
            sent.append(c)

        def arrived(d, j, sems, index, peer, core):
            b = block(d, j, core)
            copy(b, b, sems, index, peer).wait_recv()

        def onward(d):
            if plane == 4:
                send(d, 0, as_, (d,), peer_a)
                send(d, 0, bs, (2 * d,), peer_b)
            send(d, 0, ss, (d * npos,), sibling)

        for d in range(1, nz):
            send(0, 0, zs, (d,), z_peer(d))
        onward(0)
        yield
        for d in range(1, nz):
            arrived(d, 0, zs, (d,), z_peer(d), s)
            onward(d)
        yield
        if plane == 4:
            for d in range(nz):
                arrived(d, 1, as_, (d,), peer_a, s)
                send(d, 1, bs, (2 * d + 1,), peer_b)
                send(d, 1, ss, (d * npos + 1,), sibling)
            yield
            for d in range(nz):
                for j in range(2):
                    arrived(d, 2 + j, bs, (2 * d + j,), peer_b, s)
                    send(d, 2 + j, ss, (d * npos + 2 + j,), sibling)
            yield
        other = [0, 2, 1, 3] if plane == 4 else [0]
        for d in range(nz):
            for j in range(npos):
                arrived(d, other[j], ss, (d * npos + j,), sibling, 1 - s)
        for c in sent:
            c.wait_send()
        yield

    for _ in gather(tok, rows, tz, ta, tb, ts):
        pass

    mine_rows = pl.ds(pl.multiple_of(s * part, part), part)
    loads["li"].wait()
    cols = mm(tok[0, mine_rows, pl.ds(0, half)], li[pl.ds(0, half), :])
    cols += mm(tok[1, mine_rows, pl.ds(0, half)], li[pl.ds(half, half), :])
    width = li.shape[1]
    lat_t[s, pl.ds(pl.multiple_of(e * width, width), width), :] = cols.T.astype(BF16)
    going = gather(lat_t, width, lz, la, lb, ls)
    next(going)

    def shared_part(w):
        return mm(tok[0, :, pl.ds(0, half)], w[pl.ds(0, half), :]) + mm(
            tok[1, :, pl.ds(0, half)], w[pl.ds(half, half), :]
        )

    loads["sg"].wait()
    gate_s = silu(shared_part(sg))
    next(going)
    loads["su"].wait()
    if plane == 4:
        next(going)
    sh[...] = (gate_s * shared_part(su)).astype(BF16)
    w_lane = lax.broadcasted_iota(jnp.int32, (total, EXTRA), 1) == e
    w_sum = tok[0, :, pl.ds(half, EXTRA)].astype(F32) + tok[1, :, pl.ds(half, EXTRA)].astype(F32)
    w_mine = jnp.sum(jnp.where(w_lane, w_sum, 0.0), axis=1, keepdims=True)
    for _ in going:
        pass

    for h in range(2):
        lat[pl.ds(h * part, part), :] = lat_t[h].astype(F32).T.astype(BF16)
    loads["mg"].wait()
    loads["mu"].wait()
    tile = 256
    for n in range(0, hidden, tile):
        g = mm(lat[...], mg[0, :, pl.ds(n, tile)])
        u = mm(lat[...], mu[0, :, pl.ds(n, tile)])
        hid[:, pl.ds(n, tile)] = (silu(g) * u).astype(BF16)
    loads["md"].wait()
    for n in range(0, md.shape[2], tile):
        o = mm(hid[...], md[0, :, pl.ds(n, tile)]) * w_mine
        out_t[pl.ds(n, tile), :] = o.T

    def scatter_steps(own, r, S, rS, B, rB, A, rA, Z, rZ, ss, bs, as_, zs, c, finish):
        sent = []

        def block_sum(d, j):
            i = pl.ds(pl.multiple_of(at(d, j) * r, r), r)
            v = own(c, at(d, j)) + rS[c, i, :].astype(F32)
            if plane == 4:
                v += rB[c, pl.ds((2 * d + j) * r, r), :].astype(F32) if j < 2 else 0.0
                if j == 0:
                    v += rA[c, pl.ds(d * r, r), :].astype(F32)
            return v

        def push(src, dst, sems, index, peer):
            k = copy(src, dst, sems, index, peer)
            k.start()
            sent.append(k)

        def step_s():
            push(S.at[c], rS.at[c], ss, (c,), sibling)

        def step_b():
            copy(S.at[c], rS.at[c], ss, (c,), sibling).wait_recv()
            for d in range(nz):
                for j in range(2):
                    B[c, pl.ds((2 * d + j) * r, r), :] = block_sum(d, 2 + j).astype(BF16)
            push(B.at[c], rB.at[c], bs, (c,), peer_b)

        def step_a():
            copy(B.at[c], rB.at[c], bs, (c,), peer_b).wait_recv()
            for d in range(nz):
                A[c, pl.ds(d * r, r), :] = block_sum(d, 1).astype(BF16)
            push(A.at[c], rA.at[c], as_, (c,), peer_a)

        def step_z():
            if plane == 4:
                copy(A.at[c], rA.at[c], as_, (c,), peer_a).wait_recv()
            else:
                copy(S.at[c], rS.at[c], ss, (c,), sibling).wait_recv()
            for d in range(1, nz):
                Z[c, d - 1] = block_sum(d, 0).astype(BF16)
                push(Z.at[c, d - 1], rZ.at[c, d - 1], zs, (c, d - 1), z_peer(-d))

        def step_end():
            v = block_sum(0, 0)
            for d in range(1, nz):
                copy(Z.at[c, d - 1], rZ.at[c, d - 1], zs, (c, d - 1), z_peer(-d)).wait_recv()
                v += rZ[c, d - 1].astype(F32)
            finish(c, v)
            for k in sent:
                k.wait_send()

        if plane == 4:
            return [step_s, step_b, step_a, step_z, step_end]
        return [step_s, step_z, step_end]

    r = lo.shape[0]
    for i in range(n_exp):
        mS[0, pl.ds(i * r, r), :] = out_t[
            pl.ds(pl.multiple_of((2 * i + 1 - s) * r, r), r), :
        ].astype(BF16)

    def own_routed(c, i):
        return out_t[pl.ds(pl.multiple_of((2 * i + s) * r, r), r), :]

    routed = []
    steps = scatter_steps(
        own_routed, r, mS, mrS, mB, mrB, mA, mrA, mZ, mrZ, ms, mb, ma, mz, 0,
        lambda c, v: routed.append(v.T.astype(BF16)),
    )
    wide = half // chunks

    def columns(k, c):
        side = (1 - s) if k == 0 else s
        return pl.ds(pl.multiple_of(side * half + c * wide, wide), wide)

    loads["sd"].wait()
    todo = [(k, c) for c in range(chunks) for k in range(2)]
    per = -(-len(todo) // (len(steps) - 1))
    for i, step in enumerate(steps):
        step()
        for k, c in todo[i * per : (i + 1) * per]:
            partial[k, c] = mm(sh[...], sd[:, columns(k, c)])
    loads["lo"].wait()
    routed = routed[0]

    def own_mixed(c, i):
        return partial[1, c, pl.ds(pl.multiple_of(i * rows, rows), rows), :]

    def store(c, v):
        out[:, pl.ds(c * wide, wide)] = v.astype(BF16)

    plans = [
        scatter_steps(
            own_mixed, rows, fS, frS, fB, frB, fA, frA, fZ, frZ, fs, fb, fa, fz, c, store
        )
        for c in range(chunks)
    ]
    for c in range(chunks):
        fS[c] = (partial[0, c] + mm(routed, lo[:, columns(0, c)])).astype(BF16)
        plans[c][0]()
    for c in range(chunks):
        partial[1, c] = partial[1, c] + mm(routed, lo[:, columns(1, c)])
    count = len(plans[0])
    for t in range(1, count + chunks - 1):
        for c in range(chunks):
            if 1 <= t - c < count:
                plans[c][t - c]()


def per_device(n_exp, plane, *args):
    (tokens, scale, ids, latent_in, latent_out, moe_gate, moe_up, moe_down,
     shared_gate, shared_up, shared_down) = args
    rows, half = tokens.shape
    total = rows * n_exp
    latent = latent_out.shape[0] * n_exp * 2
    hidden = moe_gate.shape[2]
    nz = n_exp // plane
    chunks = 4
    wide = half // chunks
    r = latent_out.shape[0]
    two = 2 if plane == 4 else 1
    hbm = pl.BlockSpec(memory_space=pltpu.HBM)
    vmem = pl.BlockSpec(memory_space=pltpu.VMEM)

    def dma(*shape):
        return pltpu.SemaphoreType.DMA((2,) + shape)

    def scatter_buffers(n, rr, w):
        shapes = [(n, n_exp * rr, w), (n, 2 * nz * rr, w), (n, nz * rr, w), (n, max(nz - 1, 1), rr, w)]
        return [pltpu.VMEM(shape, BF16) for shape in shapes for _ in range(2)]

    return pl.pallas_call(
        functools.partial(kernel, n_exp, plane, chunks),
        out_shape=jax.ShapeDtypeStruct((rows, half), BF16),
        in_specs=[hbm, vmem, vmem] + [hbm] * 8,
        out_specs=vmem,
        scratch_shapes=[
            pltpu.VMEM((2, total, half + EXTRA), BF16),
            pltpu.VMEM(latent_in.shape, BF16),
            pltpu.VMEM(latent_out.shape, BF16),
            pltpu.VMEM(moe_gate.shape, BF16),
            pltpu.VMEM(moe_up.shape, BF16),
            pltpu.VMEM(moe_down.shape, BF16),
            pltpu.VMEM(shared_gate.shape, BF16),
            pltpu.VMEM(shared_up.shape, BF16),
            pltpu.VMEM(shared_down.shape, BF16),
            pltpu.VMEM((2, latent, total // 2), BF16),
            pltpu.VMEM((total, latent), BF16),
            pltpu.VMEM((total, hidden), BF16),
            pltpu.VMEM((total, shared_gate.shape[1]), BF16),
            pltpu.VMEM((latent, total), F32),
            pltpu.VMEM((2, chunks, total, wide), F32),
            *scatter_buffers(1, r, total),
            *scatter_buffers(chunks, rows, wide),
            pltpu.SemaphoreType.DMA((9,)),
            *[dma(nz), dma(nz), dma(2 * nz), dma(nz * plane)] * 2,
            dma(1), dma(1), dma(1), dma(1, nz),
            dma(chunks), dma(chunks), dma(chunks), dma(chunks, nz),
        ],
        compiler_params=pltpu.CompilerParams(
            collective_id=0, has_side_effects=True, vmem_limit_bytes=60 * 1024 * 1024
        ),
    )(tokens, scale, ids, latent_in, latent_out, moe_gate, moe_up, moe_down,
      shared_gate, shared_up, shared_down)


def solution(mesh):
    n_exp = mesh.shape["expert"]
    plane = 4 if mesh.shape["groups"] == 1 and n_exp % 4 == 0 else 1
    placed = (
        P(("groups", "expert"), "shard"),
        P(("groups", "expert"), None),
        P(("groups", "expert"), None),
        P(None, "expert"),
        P(("expert", "shard"), None),
        P("expert", None, "shard"),
        P("expert", None, "shard"),
        P("expert", "shard", None),
        P(None, ("expert", "shard")),
        P(None, ("expert", "shard")),
        P(("expert", "shard"), None),
    )
    return jax.shard_map(
        functools.partial(per_device, n_exp, plane),
        mesh=mesh,
        in_specs=placed,
        out_specs=P(("groups", "expert"), "shard"),
        check_vma=False,
    )
```

time: 326 us -> 82.9 us (0.25)
  waiting for transfers between devices: 231 us -> 0 us
  Pallas kernels: 0 us -> 76 us
  blocking collectives: 26.7 us -> 0 us
  matrix products: 18.7 us -> 0 us
  starting transfers between devices: 14.3 us -> 0 us
  between operations: 13.6 us -> 0.01 us
  local copies, waits for them, and re-layouts: 18.7 us -> 6.57 us
    reduce_scatter x1 -> x0, waiting for transfers between devices: 138 us -> none  [per_device(): lax.psum_scatter(arranged, ('expert', 'shard'), scatter_dimension=0, tile...]
    pallas_call x0 -> x1, Pallas kernels: none -> 76 us  [per_device(): pl.pallas_call(functools.partial(kernel, n_exp, plane, chunks), out_shape...]
    all_gather x1 -> x0, waiting for transfers between devices: 61.1 us -> none  [per_device(): every_token = lax.all_gather(full_rows, 'expert', axis=0, tiled=True)]
    all_to_all x3 -> x0, waiting for transfers between devices: 31.6 us -> none  [the longest x1 20.4 us: per_device(): lax.all_to_all(partial_value, 'expert', split_axis=0, concat_axis=0, tile...]
    dot_general x9 -> x0, matrix products: 18.7 us -> none  [the longest x1 4.84 us: per_device(): full = jnp.dot(rows, weights_cat, preferred_element_type=jnp.float32)]
    all_to_all x1 -> x0, blocking collectives: 16.2 us -> none  [per_device(): lax.all_to_all(send, 'expert', split_axis=0, concat_axis=0, tiled=True)]
    all_to_all x3 -> x0, starting transfers between devices: 14.1 us -> none  [the longest x1 6.03 us: per_device(): lax.all_to_all(routed, 'expert', split_axis=1, concat_axis=0, tiled=True)]
    transpose x1 -> x0, local copies, waits for them, and re-layouts: 7.41 us -> none  [per_device(): full.reshape(span, tok, 2, half).transpose(0, 2, 1, 3)]
  transfers between devices with their start and end apart: 5 -> 0, of which waited for: 5 -> 0; matrix products, arithmetic and copies ran while one was open for 2% -> 0% of each run, Pallas kernels for 0% -> 0%
where the time goes in v1:
time: 82.9 us; the launch traced here: 82.5 us
  Pallas kernels  76 us (92%)
  local copies, waits for them, and re-layouts  6.57 us (8%)
    pallas_call x1, Pallas kernels, per_device(): pl.pallas_call(functools.partial(kernel, n_exp, plane, chunks), out_shape...  76 us
    unnamed x4, local copies, waits for them, and re-layouts  6.57 us

profile of v1, /device:TPU:0, one launch (start us, length us, event | category | flops | bytes accessed | tf_op | source)
XLA Modules:
  0.0 82.5 jit_solution(12977650163354243574)
XLA Ops:
  0.0 1.4 %copy.12.scale = f32[16,8]{1,0:T(8,128)} copy(f32[16,8]{0,1:T(8,128)} %param.12) | data formatting | bytes 1024 | tf_op args[1]
  1.4 1.4 %copy.13.ids = s32[16,8]{1,0:T(8,128)} copy(s32[16,8]{0,1:T(8,128)} %param.13) | data formatting | bytes 1024 | tf_op args[2]
  2.7 2.4 %copy.14.latent_in = bf16[4096,64]{1,0:T(8,128)(2,1)} copy(bf16[4096,64]{0,1:T(8,128)(2,1)} %param.14) | data formatting | bytes 1048576 | tf_op args[3]
  5.1 76.0 %shard_map.109 = bf16[16,2048]{1,0:T(8,128)(2,1)} custom-call(bf16[16,2048]{1,0:T(8,128)(2,1)} %tokens.1, f32[16,8]{1,0:T(8,128)} %copy.12.scale, s32[16,8]{1,0:T(8,128)} %copy.13.ids, bf16[4096,64]{1,0:T(8,128)(2,1)} %copy.14.latent_in, bf16[32,4096]{1,0:T(8,128)(2,1)} %latent_out.1, bf16[1,1024,768]{2,1,0:T(8,128)(2,1)} %moe_gate.1, ...), custom_call_target="tpu_custom_call" | custom-call | tf_op jit(solution)/shard_map/pallas_call | solution.py:327
  81.1 1.5 %copy.16 = bf16[16,2048]{1,0:T(8,128)(2,1)} copy(bf16[16,2048]{1,0:T(8,128)(2,1)} %shard_map.109) | data formatting | bytes 131072

commit v2 on v1

--- a/solution.py
+++ b/solution.py
@@ -1,4 +1,5 @@
 import functools
+import types
 
 import jax
 import jax.numpy as jnp
@@ -10,6 +11,9 @@
 MESH = pl.DeviceIdType.MESH
 F32 = jnp.float32
 BF16 = jnp.bfloat16
+TOK_DIRECT, LAT_DIRECT, ROUTED_DIRECT, FINAL_DIRECT = True, True, True, False
+LAT_PLANE, ROUTED_PLANE = False, False
+CHUNKS = 4
 EXTRA = 128
 
 
@@ -17,8 +21,42 @@
     return jnp.dot(a, b, preferred_element_type=F32)
 
 
+def mm_t(a, b):
+    return lax.dot_general(a, b, (((1,), (1,)), ((), ())), preferred_element_type=F32)
+
+
 def silu(v):
     return v / (1.0 + jnp.exp(-v))
+
+
+def geometry(n_exp, plane, e, s):
+    nz = n_exp // plane
+    z, q = e // plane, e % plane
+    way = types.SimpleNamespace(nz=nz, npos=plane, peer_a=None, peer_b=None, peer_c=None)
+
+    def z_to(d):
+        if nz == 4:
+            return [z, z + 1 - 2 * (z % 2), z + 2 - 4 * (z // 2), 3 - z][d]
+        return lax.rem(z + d, nz)
+
+    def z_from(d):
+        return z_to(d) if nz == 4 else lax.rem(z - d + nz, nz)
+
+    spots = [q]
+    if plane == 4:
+        x, y = q % 2, q // 2
+        qx, qy = q + 1 - 2 * x, q + 2 - 4 * y
+        spots = [q, (1 - s) * qx + s * qy, (1 - s) * qy + s * qx, 3 - q]
+        way.peer_a, way.peer_b, way.peer_c = [
+            {"expert": z * plane + spot, "shard": s} for spot in spots[1:]
+        ]
+    way.at = lambda d, j: z_from(d) * plane + spots[j]
+    way.z_peer = lambda d: {"expert": z_to(d) * plane + q, "shard": s}
+    way.z_source = lambda d: {"expert": z_from(d) * plane + q, "shard": s}
+    way.peers = [way.z_peer(d) for d in range(1, nz)]
+    if plane == 4:
+        way.peers += [way.peer_a, way.peer_b, way.peer_c]
+    return way
 
 
 def kernel(
@@ -34,35 +72,18 @@
     tz, ta, tb, ts, lz, la, lb, ls,
     ms, mb, ma, mz, fs, fb, fa, fz,
 ):
-    nz = n_exp // plane
-    npos = plane
     e = lax.axis_index("expert")
     s = lax.axis_index("shard")
     rows = tokens.shape[0]
     half = tokens.shape[1]
     total = rows * n_exp
+    ids_now, scale_now = ids[...].T, scale[...].T
     part = total // 2
     hidden = mg.shape[2]
-    z, q = e // plane, e % plane
-    if plane == 4:
-        x, y = q % 2, q // 2
-        qx, qy = q + 1 - 2 * x, q + 2 - 4 * y
-        q_a = (1 - s) * qx + s * qy
-        q_b = (1 - s) * qy + s * qx
-        spots = [q, q_a, q_b, 3 - q]
-    else:
-        spots = [q]
-
-    def at(d, j):
-        return lax.rem(z - d + nz, nz) * plane + spots[j]
-
-    def z_peer(d):
-        return {"expert": lax.rem(z + d + nz, nz) * plane + q, "shard": s}
-
     sibling = {"expert": e, "shard": 1 - s}
-    if plane == 4:
-        peer_a = {"expert": z * plane + q_a, "shard": s}
-        peer_b = {"expert": z * plane + q_b, "shard": s}
+    far = geometry(n_exp, plane, e, s)
+    lat_way = far if LAT_PLANE else geometry(n_exp, 1, e, s)
+    routed_way = far if ROUTED_PLANE else geometry(n_exp, 1, e, s)
 
     loads = {}
     order = [
@@ -76,16 +97,14 @@
         loads[name].start()
 
     barrier = pltpu.get_barrier_semaphore()
-    peers = [z_peer(d) for d in range(1, nz)] + [sibling]
-    if plane == 4:
-        peers += [peer_a, peer_b]
+    peers = [sibling] + max((far, lat_way, routed_way), key=lambda way: len(way.peers)).peers
     for peer in peers:
         pl.semaphore_signal(barrier, inc=1, device_id=peer, device_id_type=MESH)
 
     lane = lax.broadcasted_iota(jnp.int32, (rows, EXTRA), 1)
     weight = jnp.zeros((rows, EXTRA), F32)
-    for k in range(ids.shape[1]):
-        weight += jnp.where(lane == ids[:, k : k + 1], scale[:, k : k + 1], 0.0)
+    for k in range(ids.shape[0]):
+        weight += jnp.where(lane == ids_now[:, k : k + 1], scale_now[:, k : k + 1], 0.0)
     high = weight.astype(BF16)
     low = (weight - high.astype(F32)).astype(BF16)
     first = jnp.broadcast_to(s, (rows, EXTRA)) == 0
@@ -100,8 +119,10 @@
             recv_sem=sems.at[(1,) + index], device_id=peer, device_id_type=MESH,
         )
 
-    def gather(buf, r, zs, as_, bs, ss):
+    def gather(buf, r, way, direct, zs, as_, bs, ss):
         sent = []
+        nz, npos, at, z_peer, z_source = way.nz, way.npos, way.at, way.z_peer, way.z_source
+        plane, peer_a, peer_b, peer_c = way.npos, way.peer_a, way.peer_b, way.peer_c
 
         def block(d, j, core):
             return buf.at[core, pl.ds(pl.multiple_of(at(d, j) * r, r), r)]
@@ -120,27 +141,43 @@
             if plane == 4:
                 send(d, 0, as_, (d,), peer_a)
                 send(d, 0, bs, (2 * d,), peer_b)
+                if direct:
+                    send(d, 0, bs, (2 * d + 1,), peer_c)
             send(d, 0, ss, (d * npos,), sibling)
+
+        def step(kind, d):
+            if kind == "z":
+                arrived(d, 0, zs, (d,), z_source(d), s)
+                onward(d)
+            elif kind == "a":
+                arrived(d, 1, as_, (d,), peer_a, s)
+                if not direct:
+                    send(d, 1, bs, (2 * d + 1,), peer_b)
+                send(d, 1, ss, (d * npos + 1,), sibling)
+            else:
+                for j in range(2):
+                    arrived(d, 2 + j, bs, (2 * d + j,), peer_c if direct and j else peer_b, s)
+                    send(d, 2 + j, ss, (d * npos + 2 + j,), sibling)
 
         for d in range(1, nz):
             send(0, 0, zs, (d,), z_peer(d))
         onward(0)
         yield
-        for d in range(1, nz):
-            arrived(d, 0, zs, (d,), z_peer(d), s)
-            onward(d)
-        yield
         if plane == 4:
-            for d in range(nz):
-                arrived(d, 1, as_, (d,), peer_a, s)
-                send(d, 1, bs, (2 * d + 1,), peer_b)
-                send(d, 1, ss, (d * npos + 1,), sibling)
+            step("a", 0)
+            step("z", 1)
+            yield
+            for d in range(2, nz):
+                step("a", d - 1)
+                step("z", d)
+            step("a", nz - 1)
             yield
             for d in range(nz):
-                for j in range(2):
-                    arrived(d, 2 + j, bs, (2 * d + j,), peer_b, s)
-                    send(d, 2 + j, ss, (d * npos + 2 + j,), sibling)
-            yield
+                step("b", d)
+        else:
+            for d in range(1, nz):
+                step("z", d)
+        yield
         other = [0, 2, 1, 3] if plane == 4 else [0]
         for d in range(nz):
             for j in range(npos):
@@ -149,16 +186,16 @@
             c.wait_send()
         yield
 
-    for _ in gather(tok, rows, tz, ta, tb, ts):
+    for _ in gather(tok, rows, far, TOK_DIRECT, tz, ta, tb, ts):
         pass
 
     mine_rows = pl.ds(pl.multiple_of(s * part, part), part)
     loads["li"].wait()
-    cols = mm(tok[0, mine_rows, pl.ds(0, half)], li[pl.ds(0, half), :])
-    cols += mm(tok[1, mine_rows, pl.ds(0, half)], li[pl.ds(half, half), :])
-    width = li.shape[1]
-    lat_t[s, pl.ds(pl.multiple_of(e * width, width), width), :] = cols.T.astype(BF16)
-    going = gather(lat_t, width, lz, la, lb, ls)
+    cols = mm_t(li[:, pl.ds(0, half)], tok[0, mine_rows, pl.ds(0, half)])
+    cols += mm_t(li[:, pl.ds(half, half)], tok[1, mine_rows, pl.ds(0, half)])
+    width = li.shape[0]
+    lat_t[s, pl.ds(pl.multiple_of(e * width, width), width), :] = cols.astype(BF16)
+    going = gather(lat_t, width, lat_way, LAT_DIRECT, lz, la, lb, ls)
     next(going)
 
     def shared_part(w):
@@ -170,8 +207,7 @@
     gate_s = silu(shared_part(sg))
     next(going)
     loads["su"].wait()
-    if plane == 4:
-        next(going)
+    next(going)
     sh[...] = (gate_s * shared_part(su)).astype(BF16)
     w_lane = lax.broadcasted_iota(jnp.int32, (total, EXTRA), 1) == e
     w_sum = tok[0, :, pl.ds(half, EXTRA)].astype(F32) + tok[1, :, pl.ds(half, EXTRA)].astype(F32)
@@ -193,13 +229,20 @@
         o = mm(hid[...], md[0, :, pl.ds(n, tile)]) * w_mine
         out_t[pl.ds(n, tile), :] = o.T
 
-    def scatter_steps(own, r, S, rS, B, rB, A, rA, Z, rZ, ss, bs, as_, zs, c, finish):
+    def scatter_steps(way, direct, own, r, S, rS, B, rB, A, rA, Z, rZ, ss, bs, as_, zs, c, finish):
         sent = []
+        nz, at, z_peer, z_source = way.nz, way.at, way.z_peer, way.z_source
+        plane, peer_a, peer_b, peer_c = way.npos, way.peer_a, way.peer_b, way.peer_c
 
         def block_sum(d, j):
             i = pl.ds(pl.multiple_of(at(d, j) * r, r), r)
             v = own(c, at(d, j)) + rS[c, i, :].astype(F32)
-            if plane == 4:
+            if plane == 4 and direct:
+                if j == 0:
+                    for k in range(2):
+                        v += rB[c, pl.ds((k * nz + d) * r, r), :].astype(F32)
+                    v += rA[c, pl.ds(d * r, r), :].astype(F32)
+            elif plane == 4:
                 v += rB[c, pl.ds((2 * d + j) * r, r), :].astype(F32) if j < 2 else 0.0
                 if j == 0:
                     v += rA[c, pl.ds(d * r, r), :].astype(F32)
@@ -218,32 +261,55 @@
             for d in range(nz):
                 for j in range(2):
                     B[c, pl.ds((2 * d + j) * r, r), :] = block_sum(d, 2 + j).astype(BF16)
-            push(B.at[c], rB.at[c], bs, (c,), peer_b)
+            push(B.at[c], rB.at[c], bs, (c, 0), peer_b)
 
         def step_a():
-            copy(B.at[c], rB.at[c], bs, (c,), peer_b).wait_recv()
+            copy(B.at[c], rB.at[c], bs, (c, 0), peer_b).wait_recv()
             for d in range(nz):
                 A[c, pl.ds(d * r, r), :] = block_sum(d, 1).astype(BF16)
             push(A.at[c], rA.at[c], as_, (c,), peer_a)
 
+        def plane_parts():
+            parts = []
+            for j, peer in ((1, peer_a), (2, peer_b), (3, peer_c)):
+                if j == 1:
+                    b, rb, sems, index = A.at[c], rA.at[c], as_, (c,)
+                else:
+                    i = pl.ds((j - 2) * nz * r, nz * r)
+                    b, rb, sems, index = B.at[c, i, :], rB.at[c, i, :], bs, (c, j - 2)
+                parts.append((j, b, rb, sems, index, peer))
+            return parts
+
+        def step_plane():
+            copy(S.at[c], rS.at[c], ss, (c,), sibling).wait_recv()
+            for j, b, rb, sems, index, peer in plane_parts():
+                for d in range(nz):
+                    b[pl.ds(d * r, r), :] = block_sum(d, j).astype(BF16)
+                push(b, rb, sems, index, peer)
+
         def step_z():
-            if plane == 4:
+            if plane == 4 and direct:
+                for j, b, rb, sems, index, peer in plane_parts():
+                    copy(b, rb, sems, index, peer).wait_recv()
+            elif plane == 4:
                 copy(A.at[c], rA.at[c], as_, (c,), peer_a).wait_recv()
             else:
                 copy(S.at[c], rS.at[c], ss, (c,), sibling).wait_recv()
             for d in range(1, nz):
                 Z[c, d - 1] = block_sum(d, 0).astype(BF16)
-                push(Z.at[c, d - 1], rZ.at[c, d - 1], zs, (c, d - 1), z_peer(-d))
+                push(Z.at[c, d - 1], rZ.at[c, d - 1], zs, (c, d - 1), z_source(d))
 
         def step_end():
             v = block_sum(0, 0)
             for d in range(1, nz):
-                copy(Z.at[c, d - 1], rZ.at[c, d - 1], zs, (c, d - 1), z_peer(-d)).wait_recv()
+                copy(Z.at[c, d - 1], rZ.at[c, d - 1], zs, (c, d - 1), z_source(d)).wait_recv()
                 v += rZ[c, d - 1].astype(F32)
             finish(c, v)
             for k in sent:
                 k.wait_send()
 
+        if plane == 4 and direct:
+            return [step_s, step_plane, step_z, step_end]
         if plane == 4:
             return [step_s, step_b, step_a, step_z, step_end]
         return [step_s, step_z, step_end]
@@ -259,7 +325,7 @@
 
     routed = []
     steps = scatter_steps(
-        own_routed, r, mS, mrS, mB, mrB, mA, mrA, mZ, mrZ, ms, mb, ma, mz, 0,
+        routed_way, ROUTED_DIRECT, own_routed, r, mS, mrS, mB, mrB, mA, mrA, mZ, mrZ, ms, mb, ma, mz, 0,
         lambda c, v: routed.append(v.T.astype(BF16)),
     )
     wide = half // chunks
@@ -286,7 +352,7 @@
 
     plans = [
         scatter_steps(
-            own_mixed, rows, fS, frS, fB, frB, fA, frA, fZ, frZ, fs, fb, fa, fz, c, store
+            far, FINAL_DIRECT, own_mixed, rows, fS, frS, fB, frB, fA, frA, fZ, frZ, fs, fb, fa, fz, c, store
         )
         for c in range(chunks)
     ]
@@ -296,10 +362,12 @@
     for c in range(chunks):
         partial[1, c] = partial[1, c] + mm(routed, lo[:, columns(1, c)])
     count = len(plans[0])
-    for t in range(1, count + chunks - 1):
-        for c in range(chunks):
-            if 1 <= t - c < count:
-                plans[c][t - c]()
+    lag = {1: 0.0, 2: 2.5, 3: 4.7}
+    turns = [
+        (c + (20 if i == count - 1 else lag[i]), i, c) for i in range(1, count) for c in range(chunks)
+    ]
+    for _, i, c in sorted(turns):
+        plans[c][i]()
 
 
 def per_device(n_exp, plane, *args):
@@ -310,7 +378,7 @@
     latent = latent_out.shape[0] * n_exp * 2
     hidden = moe_gate.shape[2]
     nz = n_exp // plane
-    chunks = 4
+    chunks = CHUNKS
     wide = half // chunks
     r = latent_out.shape[0]
     two = 2 if plane == 4 else 1
@@ -320,8 +388,8 @@
     def dma(*shape):
         return pltpu.SemaphoreType.DMA((2,) + shape)
 
-    def scatter_buffers(n, rr, w):
-        shapes = [(n, n_exp * rr, w), (n, 2 * nz * rr, w), (n, nz * rr, w), (n, max(nz - 1, 1), rr, w)]
+    def scatter_buffers(n, rr, w, last):
+        shapes = [(n, n_exp * rr, w), (n, 2 * nz * rr, w), (n, nz * rr, w), (n, last, rr, w)]
         return [pltpu.VMEM(shape, BF16) for shape in shapes for _ in range(2)]
 
     return pl.pallas_call(
@@ -331,7 +399,7 @@
         out_specs=vmem,
         scratch_shapes=[
             pltpu.VMEM((2, total, half + EXTRA), BF16),
-            pltpu.VMEM(latent_in.shape, BF16),
+            pltpu.VMEM(latent_in.shape[::-1], BF16),
             pltpu.VMEM(latent_out.shape, BF16),
             pltpu.VMEM(moe_gate.shape, BF16),
             pltpu.VMEM(moe_up.shape, BF16),
@@ -345,17 +413,17 @@
             pltpu.VMEM((total, shared_gate.shape[1]), BF16),
             pltpu.VMEM((latent, total), F32),
             pltpu.VMEM((2, chunks, total, wide), F32),
-            *scatter_buffers(1, r, total),
-            *scatter_buffers(chunks, rows, wide),
+            *scatter_buffers(1, r, total, n_exp - 1),
+            *scatter_buffers(chunks, rows, wide, nz - 1),
             pltpu.SemaphoreType.DMA((9,)),
-            *[dma(nz), dma(nz), dma(2 * nz), dma(nz * plane)] * 2,
-            dma(1), dma(1), dma(1), dma(1, nz),
-            dma(chunks), dma(chunks), dma(chunks), dma(chunks, nz),
+            *[dma(n_exp), dma(nz), dma(2 * nz), dma(n_exp)] * 2,
+            dma(1), dma(1, 2), dma(1), dma(1, n_exp),
+            dma(chunks), dma(chunks, 2), dma(chunks), dma(chunks, nz),
         ],
         compiler_params=pltpu.CompilerParams(
             collective_id=0, has_side_effects=True, vmem_limit_bytes=60 * 1024 * 1024
         ),
-    )(tokens, scale, ids, latent_in, latent_out, moe_gate, moe_up, moe_down,
+    )(tokens, scale.T, ids.T, latent_in.T, latent_out, moe_gate, moe_up, moe_down,
       shared_gate, shared_up, shared_down)
 
 

time: 82.9 us -> 68.3 us (0.82)
  Pallas kernels: 76 us -> 66.6 us
  local copies, waits for them, and re-layouts: 6.57 us -> 1.47 us
    pallas_call x1, Pallas kernels: 76 us -> 66.6 us  [per_device(): pl.pallas_call(functools.partial(kernel, n_exp, plane, chunks), out_shape...]
    unnamed x4 -> x1, local copies, waits for them, and re-layouts: 6.57 us -> 1.47 us
where the time goes in v2:
time: 68.3 us; the launch traced here: 68.1 us
  Pallas kernels  66.6 us (98%)
  local copies, waits for them, and re-layouts  1.47 us (2%)
    pallas_call x1, Pallas kernels, per_device(): pl.pallas_call(functools.partial(kernel, n_exp, plane, chunks), out_shape...  66.6 us
    unnamed x1, local copies, waits for them, and re-layouts  1.47 us

profile of v2, /device:TPU:0, one launch (start us, length us, event | category | flops | bytes accessed | tf_op | source)
XLA Modules:
  0.0 68.1 jit_solution(3541328367827250266)
XLA Ops:
  0.0 66.6 %shard_map.109 = bf16[16,2048]{1,0:T(8,128)(2,1)} custom-call(bf16[16,2048]{1,0:T(8,128)(2,1)} %tokens.1, f32[8,16]{1,0:T(8,128)} %bitcast.4, s32[8,16]{1,0:T(8,128)} %bitcast.5, bf16[64,4096]{1,0:T(8,128)(2,1)} %bitcast.3, bf16[32,4096]{1,0:T(8,128)(2,1)} %latent_out.1, bf16[1,1024,768]{2,1,0:T(8,128)(2,1)} %moe_gate.1, bf16[1,1024,768]{2,1,0:T(8,128)(2,1)} %moe_up.1, ...), custom_call_target="tpu_custom_call" | custom-call | tf_op jit(solution)/shard_map/pallas_call | solution.py:395
  66.6 1.5 %copy.13 = bf16[16,2048]{1,0:T(8,128)(2,1)} copy(bf16[16,2048]{1,0:T(8,128)(2,1)} %shard_map.109) | data formatting | bytes 131072

commit v3 on v2

--- a/solution.py
+++ b/solution.py
@@ -13,7 +13,7 @@
 BF16 = jnp.bfloat16
 TOK_DIRECT, LAT_DIRECT, ROUTED_DIRECT, FINAL_DIRECT = True, True, True, False
 LAT_PLANE, ROUTED_PLANE = False, False
-CHUNKS = 4
+CHUNKS = 2
 EXTRA = 128
 
 

time: 68.3 us -> 69.1 us (1.012)
  Pallas kernels: 66.6 us -> 67.4 us
    pallas_call x1, Pallas kernels: 66.6 us -> 67.4 us  [per_device(): pl.pallas_call(functools.partial(kernel, n_exp, plane, chunks), out_shape...]
where the time goes in v3:
time: 69.1 us; the launch traced here: 68.9 us
  Pallas kernels  67.4 us (98%)
  local copies, waits for them, and re-layouts  1.47 us (2%)
    pallas_call x1, Pallas kernels, per_device(): pl.pallas_call(functools.partial(kernel, n_exp, plane, chunks), out_shape...  67.4 us
    unnamed x1, local copies, waits for them, and re-layouts  1.47 us

profile of v3, /device:TPU:0, one launch (start us, length us, event | category | flops | bytes accessed | tf_op | source)
XLA Modules:
  0.0 68.9 jit_solution(7330540149339988725)
XLA Ops:
  0.0 67.4 %shard_map.109 = bf16[16,2048]{1,0:T(8,128)(2,1)} custom-call(bf16[16,2048]{1,0:T(8,128)(2,1)} %tokens.1, f32[8,16]{1,0:T(8,128)} %bitcast.4, s32[8,16]{1,0:T(8,128)} %bitcast.5, bf16[64,4096]{1,0:T(8,128)(2,1)} %bitcast.3, bf16[32,4096]{1,0:T(8,128)(2,1)} %latent_out.1, bf16[1,1024,768]{2,1,0:T(8,128)(2,1)} %moe_gate.1, bf16[1,1024,768]{2,1,0:T(8,128)(2,1)} %moe_up.1, ...), custom_call_target="tpu_custom_call" | custom-call | tf_op jit(solution)/shard_map/pallas_call | solution.py:395
  67.4 1.5 %copy.13 = bf16[16,2048]{1,0:T(8,128)(2,1)} copy(bf16[16,2048]{1,0:T(8,128)(2,1)} %shard_map.109) | data formatting | bytes 131072
